TPU v7x, 1024 devices: a whole 4x4x32 slice. The times are simulated.
1024 devices in a mesh: replica: 128 (over y, z_lo, x), tensor: 8 (over z_hi, core).
Axes of the slice: x: 4, y: 4, z: 32 (z_hi: 4, z_lo: 8; z = z_hi * 8 + z_lo), core: 2. Of those that a mesh axis runs over, the one named last changes fastest.
Arguments:
- attn_out: bfloat16 [131072, 3072], P('replica', 'tensor'), may hold values from -6 to 6
- w_out: bfloat16 [3072, 4096], P('tensor'), may hold values from -0.109375 to 0.109375
- local_params: bfloat16 [128, 96, 4096], P('replica', 'tensor'), may hold values from -6 to 6
- base_params: bfloat16 [96, 4096], P('tensor'), may hold values from -6 to 6
- moment: float32 [96, 4096], P('tensor'), may hold values from -4 to 4
Outputs:
- mixed: bfloat16 [131072, 4096], P(('replica', 'tensor'))
- new_params: bfloat16 [96, 4096], P('tensor')
- new_moment: float32 [96, 4096], P('tensor')
All inputs are finite; a program needn't handle non-finite values.
Results may differ from a plain program's by a relative error of at most 0.017.
Values may be sent and summed in bfloat16 or wider, within the bound.
A program may use at most 64 MiB of HBM per device.

v0:
```python
import jax
import jax.numpy as jnp
from jax import lax
from jax.sharding import PartitionSpec as P

outer_lr = 0.7
moment_coef = 0.9


def local(attn_out, w_out, local_params, base_params, moment):
    projected = lax.psum_scatter(
        jnp.dot(attn_out, w_out, preferred_element_type=jnp.float32).astype(jnp.bfloat16),
        "tensor",
        scatter_dimension=0,
        tiled=True,
    )
    base_wide = base_params.astype(jnp.float32)
    rounded = lax.optimization_barrier(
        (base_wide - local_params[0].astype(jnp.float32)).astype(jnp.bfloat16)
    )
    replicas = lax.axis_size("replica")
    summed = lax.psum(rounded.astype(jnp.float32), "replica")
    outer_grad = summed / replicas
    new_moment = moment_coef * moment + outer_grad
    new_params = (base_wide - outer_lr * (outer_grad + moment_coef * new_moment)).astype(
        jnp.bfloat16
    )
    return (projected, new_params, new_moment)


def solution(mesh):
    in_specs = (
        P("replica", "tensor"),
        P("tensor", None),
        P("replica", "tensor", None),
        P("tensor", None),
        P("tensor", None),
    )
    out_specs = (P(("replica", "tensor"), None), P("tensor", None), P("tensor", None))
    return jax.shard_map(local, mesh=mesh, in_specs=in_specs, out_specs=out_specs, check_vma=False)
```

profile of v0, /device:TPU:256, one launch (start us, length us, event | category | flops | bytes accessed | tf_op | source)
XLA Modules:
  0.0 1341.6 jit_solution(6695993351395940879)
XLA Ops:
  7.2 0.0 copy-start
  7.2 0.0 reduce-scatter.2.cloned.1.call-start
  7.2 1.8 copy-done
  9.1 7.8 convolution_convert_fusion
  16.9 0.0 copy-start.1
  16.9 0.0 copy-start.2
  16.9 0.0 reduce-scatter.2.cloned.1.call-update
  16.9 0.9 copy-done.1
  17.8 0.1 copy-done.2
  17.9 1315.1 %all-reduce.1 = f32[12,4096]{1,0:T(8,128)S(1)} all-reduce(bf16[12,4096]{1,0:T(8,128)(2,1)S(1)} %fusion), channel_id=1, replica_groups=mesh['replica'=128,'tensor'=8] {'replica'}, use_global_device_ids=true, to_apply=%region_1.0 | all-reduce | flops 49152 | bytes 294912 | tf_op jit(solution)/shard_map/psum | solution.py:22
  1333.0 1.8 fusion.1
  1334.8 0.0 reduce-scatter.2.cloned.1.call-done
  (1 shorter events, 0.0 us)
Async XLA Ops:
  7.2 1.9 copy-start
  7.2 1327.6 %reduce-scatter.2.cloned.1.call-start = ((), (), s32[]{:S(2)}) async-start(), calls=%async_computation.1 | async-start | bytes 9437184 | tf_op jit(solution)/shard_map/reduce_scatter | solution.py:11
  16.9 0.9 copy-start.1
  16.9 1.0 copy-start.2
Sparse Core Ops, SparseCore 0:
  17.0 352.1 reduce-scatter.1
where the time goes:
time: 1340 us
  blocking collectives  1320 us (99%)
  between operations  14 us (1%)
    psum x1, blocking collectives, local(): summed = lax.psum(rounded.astype(jnp.float32), 'replica')  1320 us
  transfers between devices with their start and end apart: 1, of which 0 were waited for; matrix products, arithmetic and copies ran while one was open for 0% of the time, Pallas kernels for 0%

commit v1 on v0

v1 whole, which is shorter than its diff:
```python
import jax
import jax.numpy as jnp
from jax import lax
from jax.experimental import pallas as pl
from jax.experimental.pallas import tpu as pltpu
from jax.sharding import PartitionSpec as P

MESH = pl.DeviceIdType.MESH
outer_lr = 0.7
moment_coef = 0.9

PIECES = 8
ROWS = 48
COLS = 256
BLOCKS = 16
OFFSETS = (0, -1, 1, 2)
ROUNDS = PIECES + 3


def kernel(
    attn, w, local_params, base, moment, out, new_params, new_moment,
    wall, own, heads, relay, acc, give, take, diff, diffs, zsum, ztake, grad,
    local_sem, first_send, first_recv, win_send, win_recv, plane_send, plane_recv,
    attn_send, attn_recv, diff_send, diff_recv, z_send, z_recv, grad_send, grad_recv, half_send, half_recv,
):
    replica, tensor = lax.axis_index("replica"), lax.axis_index("tensor")
    x, z_lo, y = lax.rem(replica, 4), lax.rem(lax.div(replica, 4), 8), lax.div(replica, 32)
    z_hi, core = lax.div(tensor, 2), lax.rem(tensor, 2)
    z = z_hi * 8 + z_lo
    mine = y * 4 + x

    def device(x, y, z, core):
        x, y, z = lax.rem(x + 8, 4), lax.rem(y + 8, 4), lax.rem(z + 64, 32)
        return {
            "replica": (y * 8 + lax.rem(z, 8)) * 4 + x,
            "tensor": lax.div(z, 8) * 2 + core,
        }

    def copy(source, target, send, recv, to):
        return pltpu.make_async_remote_copy(
            src_ref=source, dst_ref=target, send_sem=send, recv_sem=recv, device_id=to, device_id_type=MESH
        )

    columns = pl.ds(pl.multiple_of(mine * COLS, COLS), COLS)
    locals_ = [
        pltpu.make_async_copy(w.at[:, :, columns], wall.at[mine, :, 0], local_sem.at[0]),
        pltpu.make_async_copy(w.at[:, :, columns], wall.at[mine, :, 4], local_sem.at[1]),
        pltpu.make_async_copy(w, own, local_sem.at[2]),
        pltpu.make_async_copy(attn.at[pl.ds(pl.multiple_of(z_hi * 256, 256), 256)], heads.at[0], local_sem.at[3]),
    ]
    for one in locals_:
        one.start()

    def z_partner(step):
        bit = 1 << step
        return z + bit - 2 * bit * lax.rem(lax.div(z_lo, bit), 2)

    partners = [device(x + j % 4, y + j // 4, z, core) for j in range(1, 16)]
    partners += [device(x, y, z + 1, core), device(x, y, z - 1, core)]
    partners += [device(x, y, z + 8 * j, core) for j in (1, 2, 3)]
    partners += [device(x, y, z_partner(step), core) for step in (1, 2)]
    sibling = device(x, y, z, 1 - core)
    partners += [sibling]
    barrier = pltpu.get_barrier_semaphore()
    for one in partners:
        pl.semaphore_signal(barrier, inc=1, device_id=one, device_id_type=MESH)

    diff[...] = jnp.zeros_like(diff)

    @pl.loop(0, BLOCKS)
    def _(block):
        at = pl.ds(pl.multiple_of(block * COLS, COLS), COLS)
        wide = base[:, at].astype(jnp.float32) - local_params[:, at].astype(jnp.float32)
        diff[block, 0:12, :] = wide.astype(jnp.bfloat16)

    locals_[0].wait()
    locals_[1].wait()
    pl.semaphore_wait(barrier, len(partners))

    firsts = []
    for j in (1, 2, 3):
        firsts.append(
            copy(
                wall.at[mine, z_lo, 0], wall.at[mine, z_lo, 4 - j],
                first_send.at[j - 1], first_recv.at[3 - j], device(x, y, z + 8 * j, core),
            )
        )
        firsts[-1].start()

    diff_copies = []
    for j in range(1, 16):
        dx, dy = j % 4, j // 4
        block = lax.rem(y + dy, 4) * 4 + lax.rem(x + dx, 4)
        diff_copies.append(
            copy(
                diff.at[block], diffs.at[j - 1], diff_send.at[j - 1], diff_recv.at[j - 1],
                device(x + dx, y + dy, z, core),
            )
        )
        diff_copies[-1].start()

    def rows_of(j, start, size):
        return attn.at[pl.ds(pl.multiple_of(lax.rem(z_hi + j, 4) * 256 + start, 128), size)]

    up, down = device(x, y, z + 8, core), device(x, y, z - 8, core)
    attn_copies = [
        copy(rows_of(2, 0, 128), relay.at[0], attn_send.at[0], attn_recv.at[0], up),
        copy(rows_of(2, 128, 128), relay.at[1], attn_send.at[1], attn_recv.at[1], down),
        copy(rows_of(1, 0, 256), heads.at[3], attn_send.at[2], attn_recv.at[2], up),
        copy(rows_of(3, 0, 256), heads.at[1], attn_send.at[3], attn_recv.at[3], down),
    ]
    for one in attn_copies:
        one.start()
    relays = [
        copy(relay.at[0], heads.at[2, pl.ds(0, 128)], attn_send.at[4], attn_recv.at[4], up),
        copy(relay.at[1], heads.at[2, pl.ds(128, 128)], attn_send.at[5], attn_recv.at[5], down),
    ]

    def piece_of(n):
        away = lax.div(n + 1, 2)
        return lax.rem(z_lo + jnp.where(lax.rem(n, 2) == 1, 8 - away, away), 8)

    def window(piece, n, upward):
        if upward:
            start, to = 1 + lax.div(z_lo, 7), device(x, y, z + 1, core)
        else:
            start, to = 1 - lax.div(7 - z_lo, 7), device(x, y, z - 1, core)
        return copy(
            wall.at[mine, piece, pl.ds(start, 3)], wall.at[mine, piece, pl.ds(1, 3)],
            win_send.at[n - 1], win_recv.at[n - 1], to,
        )

    def plane(n, piece, a, b, to_a, to_b, which):
        first_x = 1 - lax.rem(n, 2)
        sx, sy = a * first_x + b * (1 - first_x), b * first_x + a * (1 - first_x)
        tx, ty = to_a * first_x + to_b * (1 - first_x), to_b * first_x + to_a * (1 - first_x)
        block = lax.rem(y + sy + 4, 4) * 4 + lax.rem(x + sx + 4, 4)
        part = wall.at[block, piece, pl.ds(1, 3)]
        index = n * 15 + which
        return copy(part, part, plane_send.at[index], plane_recv.at[index], device(x + tx, y + ty, z, core))

    def spread(n, piece, i):
        plane(n, piece, OFFSETS[i], 0, 0, 1, 3 + 3 * i).start()
        plane(n, piece, OFFSETS[i], 0, 0, -1, 4 + 3 * i).start()

    def arrive(n, which):
        part = wall.at[mine, 0, pl.ds(1, 3)]
        index = n * 15 + which
        copy(part, part, plane_send.at[index], plane_recv.at[index], sibling).wait_recv()

    def stage0(n):
        piece = piece_of(n)

        @pl.when(n >= 1)
        def _():
            window(piece, n, True).wait_recv()

        @pl.when(n == 0)
        def _():
            window(piece, n + 1, True).start()

        @pl.when(n <= 5)
        def _():
            @pl.when(lax.rem(n, 2) == 1)
            def _():
                window(piece, n + 2, True).start()

            @pl.when(lax.rem(n, 2) == 0)
            def _():
                window(piece, n + 2, False).start()

        plane(n, piece, 0, 0, 1, 0, 0).start()
        plane(n, piece, 0, 0, -1, 0, 1).start()
        spread(n, piece, 0)

    def stage1(n):
        piece = piece_of(n)
        route = lax.rem(lax.div(n, 2), 2)
        arrive(n, 0)

        @pl.when(route == 0)
        def _():
            plane(n, piece, -1, 0, 1, 0, 2).start()

        spread(n, piece, 1)
        arrive(n, 1)

        @pl.when(route == 1)
        def _():
            plane(n, piece, 1, 0, -1, 0, 2).start()

        spread(n, piece, 2)

    def stage2(n):
        piece = piece_of(n)
        arrive(n, 2)
        spread(n, piece, 3)

    def stage3(n):
        piece = piece_of(n)
        for i in range(4):
            arrive(n, 3 + 3 * i)
            if i % 2 == 0:
                plane(n, piece, OFFSETS[i], -1, 0, 1, 5 + 3 * i).start()
            arrive(n, 4 + 3 * i)
            if i % 2 == 1:
                plane(n, piece, OFFSETS[i], 1, 0, -1, 5 + 3 * i).start()

    for one in firsts:
        one.wait_recv()

    z_copies = [
        copy(zsum.at[step], ztake.at[step], z_send.at[step], z_recv.at[step], device(x, y, z_partner(step), core))
        for step in range(3)
    ]
    grad_copies = []
    for j in range(1, 16):
        grad_copies.append(
            copy(
                zsum.at[3], grad.at[mine], grad_send.at[j - 1], grad_recv.at[j - 1],
                device(x + j % 4, y + j // 4, z, core),
            )
        )

    @pl.loop(0, ROUNDS)
    def _(m):
        @pl.when(m < PIECES)
        def _():
            stage0(m)

        @pl.when((m >= 1) & (m < PIECES + 1))
        def _():
            stage1(m - 1)

        @pl.when((m >= 2) & (m < PIECES + 2))
        def _():
            stage2(m - 2)

        @pl.when(m >= 3)
        def _():
            stage3(m - 3)

        @pl.when(m == 1)
        def _():
            for one in diff_copies:
                one.wait_recv()
            total = diff[mine].astype(jnp.float32)
            for j in range(15):
                total = total + diffs[j].astype(jnp.float32)
            zsum[0] = total
            z_copies[0].start()

        for step in range(3):

            @pl.when(m == 2 + step)
            def _(step=step):
                z_copies[step].wait_recv()
                zsum[step + 1] = zsum[step] + ztake[step]
                if step < 2:
                    z_copies[step + 1].start()
                else:
                    grad[mine] = zsum[3]
                    for one in grad_copies:
                        one.start()

        @pl.when(m == 3)
        def _():
            for index in (0, 1):
                attn_copies[index].wait_recv()
                relays[index].start()

    @pl.loop(0, PIECES)
    def _(n):
        for i in range(4):
            arrive(n, 5 + 3 * i)

    for one in grad_copies:
        one.wait_recv()

    @pl.loop(0, BLOCKS)
    def _(block):
        at = pl.ds(pl.multiple_of(block * COLS, COLS), COLS)
        outer_grad = grad[block, 0:12, :] / 128
        moved = moment_coef * moment[:, at] + outer_grad
        new_moment[:, at] = moved
        new_params[:, at] = (
            base[:, at].astype(jnp.float32) - outer_lr * (outer_grad + moment_coef * moved)
        ).astype(jnp.bfloat16)

    def part(index, block):
        return jnp.dot(
            heads[index], wall[block, :, index].reshape(PIECES * ROWS, COLS), preferred_element_type=jnp.float32
        )

    locals_[2].wait()
    locals_[3].wait()

    @pl.loop(0, BLOCKS)
    def _(block):
        at = pl.ds(pl.multiple_of(block * COLS, COLS), COLS)
        acc[block] = jnp.dot(
            heads[0], own[:, :, at].reshape(PIECES * ROWS, COLS), preferred_element_type=jnp.float32
        )

    attn_copies[2].wait_recv()
    attn_copies[3].wait_recv()

    @pl.loop(0, BLOCKS)
    def _(block):
        acc[block] += part(1, block) + part(3, block)

    relays[0].wait_recv()
    relays[1].wait_recv()
    kept = pl.ds(pl.multiple_of(core * 128, 128), 128)
    given = pl.ds(pl.multiple_of((1 - core) * 128, 128), 128)

    def half(block):
        return copy(give.at[block], take.at[block], half_send.at[block], half_recv.at[block], sibling)

    @pl.loop(0, BLOCKS)
    def _(block):
        acc[block] += part(2, block)
        give[block] = acc[block, given, :].astype(jnp.bfloat16)
        half(block).start()

    @pl.loop(0, BLOCKS)
    def _(block):
        at = pl.ds(pl.multiple_of(block * COLS, COLS), COLS)
        half(block).wait_recv()
        out[:, at] = (acc[block, kept, :] + take[block].astype(jnp.float32)).astype(jnp.bfloat16)

    @pl.loop(0, PIECES * 15)
    def _(index):
        part_ = wall.at[mine, 0, pl.ds(1, 3)]
        copy(part_, part_, plane_send.at[index], plane_recv.at[index], sibling).wait_send()

    @pl.loop(0, BLOCKS)
    def _(block):
        half(block).wait_send()

    for n in range(1, 8):
        window(0, n, True).wait_send()
    for one in firsts + diff_copies + attn_copies + relays + z_copies + grad_copies:
        one.wait_send()


def local(attn_out, w_out, local_params, base_params, moment):
    vmem, hbm = pl.BlockSpec(memory_space=pltpu.VMEM), pl.BlockSpec(memory_space=pl.ANY)
    dma = pltpu.SemaphoreType.DMA
    bf16, f32 = jnp.bfloat16, jnp.float32
    return pl.pallas_call(
        kernel,
        out_shape=(
            jax.ShapeDtypeStruct((128, 4096), bf16),
            jax.ShapeDtypeStruct((12, 4096), bf16),
            jax.ShapeDtypeStruct((12, 4096), f32),
        ),
        in_specs=[hbm, hbm, vmem, vmem, vmem],
        out_specs=(vmem, vmem, vmem),
        scratch_shapes=[
            pltpu.VMEM((BLOCKS, PIECES, 5, ROWS, COLS), bf16),
            pltpu.VMEM((PIECES, ROWS, 4096), bf16),
            pltpu.VMEM((4, 256, 384), bf16),
            pltpu.VMEM((2, 128, 384), bf16),
            pltpu.VMEM((BLOCKS, 256, COLS), f32),
            pltpu.VMEM((BLOCKS, 128, COLS), bf16),
            pltpu.VMEM((BLOCKS, 128, COLS), bf16),
            pltpu.VMEM((BLOCKS, 16, COLS), bf16),
            pltpu.VMEM((15, 16, COLS), bf16),
            pltpu.VMEM((4, 16, COLS), f32),
            pltpu.VMEM((3, 16, COLS), f32),
            pltpu.VMEM((BLOCKS, 16, COLS), f32),
            dma((4,)),
            dma((3,)),
            dma((3,)),
            dma((7,)),
            dma((7,)),
            dma((PIECES * 15,)),
            dma((PIECES * 15,)),
            dma((6,)),
            dma((6,)),
            dma((15,)),
            dma((15,)),
            dma((3,)),
            dma((3,)),
            dma((15,)),
            dma((15,)),
            dma((BLOCKS,)),
            dma((BLOCKS,)),
        ],
        compiler_params=pltpu.CompilerParams(
            collective_id=0, has_side_effects=True, vmem_limit_bytes=56 * 1024 * 1024
        ),
        cost_estimate=pl.CostEstimate(flops=2 * 256 * 1536 * 4096, bytes_accessed=8 << 20, transcendentals=0),
    )(attn_out, w_out.reshape(PIECES, ROWS, 4096), local_params.reshape(12, 4096), base_params, moment)


def solution(mesh):
    in_specs = (
        P("replica", "tensor"),
        P("tensor", None),
        P("replica", "tensor", None),
        P("tensor", None),
        P("tensor", None),
    )
    out_specs = (P(("replica", "tensor"), None), P("tensor", None), P("tensor", None))
    return jax.shard_map(local, mesh=mesh, in_specs=in_specs, out_specs=out_specs, check_vma=False)
```

time: 1340 us -> 174 us (0.13)
  the two profiles are of different devices: /device:TPU:256 before, /device:TPU:3 now
where the time goes in v1:
time: 174 us
  Pallas kernels  168 us (97%)
  local copies, waits for them, and re-layouts  5.52 us (3%)
    pallas_call x1, Pallas kernels, local(): pl.pallas_call(kernel, out_shape=(jax.ShapeDtypeStruct((128, 4096), bf16)...  168 us
    unnamed x3, local copies, waits for them, and re-layouts  5.52 us

profile of v1, /device:TPU:3, one launch (start us, length us, event | category | flops | bytes accessed | tf_op | source)
XLA Modules:
  0.0 173.8 jit_solution(15111028130312638409)
XLA Ops:
  0.6 167.7 %shard_map.76 = (bf16[128,4096]{1,0:T(8,128)(2,1)}, bf16[12,4096]{1,0:T(8,128)(2,1)}, f32[12,4096]{1,0:T(8,128)}) custom-call(bf16[1024,384]{1,0:T(8,128)(2,1)} %attn.1, bf16[8,48,4096]{2,1,0:T(8,128)(2,1)} %bitcast.2, bf16[12,4096]{1,0:T(8,128)(2,1)} %bitcast.3, bf16[12,4096]{1,0:T(8,128)(2,1)} %base.1, f32[12,4096]{1,0:T(8,128)} %moment.1), custom_call_target="tpu_custom_call" | custom-call | flops 3221225472 | bytes 8388608 | tf_op jit(solution)/shard_map/pallas_call | solution.py:351
  168.3 2.3 %copy.11 = bf16[128,4096]{1,0:T(8,128)(2,1)} copy(bf16[128,4096]{1,0:T(8,128)(2,1)} %get-tuple-element.6) | data formatting | bytes 2097152
  170.6 1.6 copy.12
  172.1 1.7 copy.13

commit v2 on v1

v2 whole, which is shorter than its diff:
```python
import jax
import jax.numpy as jnp
from jax import lax
from jax.experimental import pallas as pl
from jax.experimental.pallas import tpu as pltpu
from jax.sharding import PartitionSpec as P

MESH = pl.DeviceIdType.MESH
outer_lr = 0.7
moment_coef = 0.9

PIECES = 8
ROWS = 48
COLS = 256
BLOCKS = 16
OFFSETS = (0, -1, 1, 2)
ROUNDS = PIECES + 2
FAR_STEPS = (0, 1, 2, 3)
NEAR_STEPS = (5, 6, 7, 8)
UNROLL = 1
RELAY_ROUNDS = (0, 1, 2, 3)
PARTS = len(FAR_STEPS)


def kernel(
    attn, w, local_params, base, out, summed,
    wall, own, heads, relay, acc, give, take, diff, diffs, zsum, ztake, grad,
    local_sem, first_send, first_recv, win_send, win_recv, plane_send, plane_recv,
    near_send, near_recv, far_send, far_recv, relay_send, relay_recv, diff_send, diff_recv, z_send, z_recv, grad_send, grad_recv, half_send, half_recv,
):
    replica, tensor = lax.axis_index("replica"), lax.axis_index("tensor")
    x, z_lo, y = lax.rem(replica, 4), lax.rem(lax.div(replica, 4), 8), lax.div(replica, 32)
    z_hi, core = lax.div(tensor, 2), lax.rem(tensor, 2)
    z = z_hi * 8 + z_lo
    mine = y * 4 + x

    def device(x, y, z, core):
        x, y, z = lax.rem(x + 8, 4), lax.rem(y + 8, 4), lax.rem(z + 64, 32)
        return {
            "replica": (y * 8 + lax.rem(z, 8)) * 4 + x,
            "tensor": lax.div(z, 8) * 2 + core,
        }

    def copy(source, target, send, recv, to):
        return pltpu.make_async_remote_copy(
            src_ref=source, dst_ref=target, send_sem=send, recv_sem=recv, device_id=to, device_id_type=MESH
        )

    columns = pl.ds(pl.multiple_of(mine * COLS, COLS), COLS)
    locals_ = [
        pltpu.make_async_copy(w.at[:, :, columns], wall.at[mine, :, 0], local_sem.at[0]),
        pltpu.make_async_copy(w.at[:, :, columns], wall.at[mine, :, 4], local_sem.at[1]),
        pltpu.make_async_copy(w, own, local_sem.at[2]),
        pltpu.make_async_copy(attn.at[pl.ds(pl.multiple_of(z_hi * 256, 256), 256)], heads.at[0], local_sem.at[3]),
    ]
    for one in locals_:
        one.start()

    def z_partner(step):
        bit = 1 << step
        return z + bit - 2 * bit * lax.rem(lax.div(z_lo, bit), 2)

    partners = [device(x + j % 4, y + j // 4, z, core) for j in range(1, 16)]
    partners += [device(x, y, z + 1, core), device(x, y, z - 1, core)]
    partners += [device(x, y, z + 8 * j, core) for j in (1, 2, 3)]
    partners += [device(x, y, z_partner(step), core) for step in (1, 2)]
    sibling = device(x, y, z, 1 - core)
    partners += [sibling]
    barrier = pltpu.get_barrier_semaphore()
    for one in partners:
        pl.semaphore_signal(barrier, inc=1, device_id=one, device_id_type=MESH)

    pl.semaphore_wait(barrier, len(partners))

    firsts = []
    for j in (1, 2, 3):
        firsts.append(
            copy(
                w.at[z_lo, :, columns], wall.at[mine, z_lo, 4 - j],
                first_send.at[j - 1], first_recv.at[3 - j], device(x, y, z + 8 * j, core),
            )
        )
        firsts[-1].start()

    diff[...] = jnp.zeros_like(diff)

    @pl.loop(0, BLOCKS)
    def _(block):
        at = pl.ds(pl.multiple_of(block * COLS, COLS), COLS)
        wide = base[:, at].astype(jnp.float32) - local_params[:, at].astype(jnp.float32)
        diff[block, 0:12, :] = wide.astype(jnp.bfloat16)

    diff_copies = []
    for j in range(1, 16):
        dx, dy = j % 4, j // 4
        block = lax.rem(y + dy, 4) * 4 + lax.rem(x + dx, 4)
        diff_copies.append(
            copy(
                diff.at[block], diffs.at[j - 1], diff_send.at[j - 1], diff_recv.at[j - 1],
                device(x + dx, y + dy, z, core),
            )
        )
        diff_copies[-1].start()

    def rows_of(j, start, size):
        return attn.at[pl.ds(pl.multiple_of(lax.rem(z_hi + j, 4) * 256 + start, 16), size)]

    up, down = device(x, y, z + 8, core), device(x, y, z - 8, core)
    high = 128 // PARTS
    far_copies, relays = [], []
    for k in range(PARTS):
        for side, to in enumerate((up, down)):
            held = relay.at[side, pl.ds(k * high, high)]
            landing = heads.at[2, pl.ds(side * 128 + k * high, high)]
            index = 2 * k + side
            far_copies.append(
                copy(rows_of(2, side * 128 + k * high, high), held, far_send.at[index], far_recv.at[index], to)
            )
            relays.append(copy(held, landing, relay_send.at[index], relay_recv.at[index], to))
    near_copies = []
    for k in range(PARTS):
        part_rows = pl.ds(k * 64, 64)
        near_copies += [
            copy(rows_of(1, k * 64, 64), heads.at[3, part_rows], near_send.at[2 * k], near_recv.at[2 * k], up),
            copy(rows_of(3, k * 64, 64), heads.at[1, part_rows], near_send.at[2 * k + 1], near_recv.at[2 * k + 1], down),
        ]

    def piece_of(n):
        away = (n + 1) // 2
        odd = n % 2
        return lax.rem(z_lo + odd * (8 - away) + (1 - odd) * away, 8)

    def window(piece, n, upward):
        if upward:
            start, to = 1 + lax.div(z_lo, 7), device(x, y, z + 1, core)
        else:
            start, to = 1 - lax.div(7 - z_lo, 7), device(x, y, z - 1, core)
        return copy(
            wall.at[mine, piece, pl.ds(start, 3)], wall.at[mine, piece, pl.ds(1, 3)],
            win_send.at[n - 1], win_recv.at[n - 1], to,
        )

    def plane(n, piece, a, b, to_a, to_b, which):
        first_x = 1 - n % 2
        sx, sy = a * first_x + b * (1 - first_x), b * first_x + a * (1 - first_x)
        tx, ty = to_a * first_x + to_b * (1 - first_x), to_b * first_x + to_a * (1 - first_x)
        block = lax.rem(y + sy + 4, 4) * 4 + lax.rem(x + sx + 4, 4)
        part = wall.at[block, piece, pl.ds(1, 3)]
        index = n * 15 + which
        return copy(part, part, plane_send.at[index], plane_recv.at[index], device(x + tx, y + ty, z, core))

    def spread(n, piece, i):
        plane(n, piece, OFFSETS[i], 0, 0, 1, 3 + 3 * i).start()
        plane(n, piece, OFFSETS[i], 0, 0, -1, 4 + 3 * i).start()

    def arrive(n, which):
        part = wall.at[mine, 0, pl.ds(1, 3)]
        index = n * 15 + which
        copy(part, part, plane_send.at[index], plane_recv.at[index], sibling).wait_recv()

    def window_take(n, upward):
        piece = piece_of(n)
        window(piece, n, upward).wait_recv()

        if n + 2 < PIECES:
            window(piece, n + 2, upward).start()

        stage0(n)

    def stage0(n):
        piece = piece_of(n)
        plane(n, piece, 0, 0, 1, 0, 0).start()
        plane(n, piece, 0, 0, -1, 0, 1).start()
        spread(n, piece, 0)

    def stage1(n):
        piece = piece_of(n)
        route = lax.rem(lax.div(n, 2), 2)
        arrive(n, 0)

        @pl.when(route == 0)
        def _():
            plane(n, piece, -1, 0, 1, 0, 2).start()

        spread(n, piece, 1)
        arrive(n, 1)

        @pl.when(route == 1)
        def _():
            plane(n, piece, 1, 0, -1, 0, 2).start()

        spread(n, piece, 2)

    def stage2(n):
        piece = piece_of(n)
        arrive(n, 2)
        spread(n, piece, 3)

    def stage3(n, i):
        piece = piece_of(n)
        arrive(n, 3 + 3 * i)
        if i % 2 == 0:
            plane(n, piece, OFFSETS[i], -1, 0, 1, 5 + 3 * i).start()
        arrive(n, 4 + 3 * i)
        if i % 2 == 1:
            plane(n, piece, OFFSETS[i], 1, 0, -1, 5 + 3 * i).start()

    z_copies = [
        copy(zsum.at[step], ztake.at[step], z_send.at[step], z_recv.at[step], device(x, y, z_partner(step), core))
        for step in range(3)
    ]
    grad_copies = []
    for j in range(1, 16):
        grad_copies.append(
            copy(
                zsum.at[3], grad.at[mine], grad_send.at[j - 1], grad_recv.at[j - 1],
                device(x + j % 4, y + j // 4, z, core),
            )
        )

    def attn_step(m):
        for k in range(PARTS):
            if m == FAR_STEPS[k]:
                far_copies[2 * k].start()
                far_copies[2 * k + 1].start()
        for k in range(PARTS):
            if m == NEAR_STEPS[k]:
                near_copies[2 * k].start()
                near_copies[2 * k + 1].start()

    def sum_step(step):
        z_copies[step].wait_recv()
        zsum[step + 1] = zsum[step] + ztake[step]
        if step < 2:
            z_copies[step + 1].start()
        else:
            grad[mine] = zsum[3]
            for one in grad_copies:
                one.start()

    attn_step(0)
    for one in diff_copies:
        one.wait_recv()
    total = diff[mine].astype(jnp.float32)
    for j in range(15):
        total = total + diffs[j].astype(jnp.float32)
    zsum[0] = total
    z_copies[0].start()
    sum_step(0)
    locals_[0].wait()
    locals_[1].wait()
    for one in firsts:
        one.wait_recv()
    window(z_lo, 1, True).start()
    window(z_lo, 2, False).start()
    stage0(0)
    sum_step(1)
    attn_step(1)
    locals_[2].wait()
    locals_[3].wait()

    @pl.loop(0, BLOCKS, unroll=UNROLL)
    def _(block):
        at = pl.ds(pl.multiple_of(block * COLS, COLS), COLS)
        acc[block] = jnp.dot(
            heads[0], own[:, :, at].reshape(PIECES * ROWS, COLS), preferred_element_type=jnp.float32
        )

    for step in range(3):
        window_take(2 * step + 1, True)
        window_take(2 * step + 2, False)
        if step == 0:
            sum_step(2)
        attn_step(2 + step)
    window_take(7, True)
    attn_step(5)

    @pl.loop(0, ROUNDS)
    def _(m):
        @pl.when(m < PIECES)
        def _():
            stage1(m)
            stage3(m, 0)

        @pl.when((m >= 1) & (m < PIECES + 1))
        def _():
            stage2(m - 1)
            stage3(m - 1, 1)
            stage3(m - 1, 2)

        @pl.when(m >= 2)
        def _():
            stage3(m - 2, 3)

        for k in range(PARTS):
            if NEAR_STEPS[k] >= 6:

                @pl.when(m == NEAR_STEPS[k] - 6)
                def _(k=k):
                    near_copies[2 * k].start()
                    near_copies[2 * k + 1].start()

            @pl.when(m == RELAY_ROUNDS[k])
            def _(k=k):
                for index in (2 * k, 2 * k + 1):
                    far_copies[index].wait_recv()
                    relays[index].start()

    @pl.loop(0, PIECES)
    def _(n):
        for i in range(4):
            arrive(n, 5 + 3 * i)

    for one in grad_copies:
        one.wait_recv()

    @pl.loop(0, BLOCKS)
    def _(block):
        at = pl.ds(pl.multiple_of(block * COLS, COLS), COLS)
        summed[:, at] = grad[block, 0:12, :]

    def part(index, block):
        return jnp.dot(
            heads[index], wall[block, :, index].reshape(PIECES * ROWS, COLS), preferred_element_type=jnp.float32
        )

    for one in near_copies:
        one.wait_recv()

    @pl.loop(0, BLOCKS, unroll=UNROLL)
    def _(block):
        acc[block] += part(1, block) + part(3, block)

    for one in relays:
        one.wait_recv()
    kept = pl.ds(pl.multiple_of(core * 128, 128), 128)
    given = pl.ds(pl.multiple_of((1 - core) * 128, 128), 128)

    def half(block):
        return copy(give.at[block], take.at[block], half_send.at[block], half_recv.at[block], sibling)

    @pl.loop(0, BLOCKS, unroll=UNROLL)
    def _(block):
        acc[block] += part(2, block)
        give[block] = acc[block, given, :].astype(jnp.bfloat16)
        half(block).start()

    @pl.loop(0, BLOCKS, unroll=UNROLL)
    def _(block):
        at = pl.ds(pl.multiple_of(block * COLS, COLS), COLS)
        half(block).wait_recv()
        out[:, at] = (acc[block, kept, :] + take[block].astype(jnp.float32)).astype(jnp.bfloat16)

    @pl.loop(0, PIECES * 15)
    def _(index):
        part_ = wall.at[mine, 0, pl.ds(1, 3)]
        copy(part_, part_, plane_send.at[index], plane_recv.at[index], sibling).wait_send()

    @pl.loop(0, BLOCKS)
    def _(block):
        half(block).wait_send()

    for n in range(1, 8):
        window(0, n, True).wait_send()
    for one in firsts + diff_copies + near_copies + far_copies + relays + z_copies + grad_copies:
        one.wait_send()


def local(attn_out, w_out, local_params, base_params, moment):
    vmem, hbm = pl.BlockSpec(memory_space=pltpu.VMEM), pl.BlockSpec(memory_space=pl.ANY)
    dma = pltpu.SemaphoreType.DMA
    bf16, f32 = jnp.bfloat16, jnp.float32
    projected, summed = pl.pallas_call(
        kernel,
        out_shape=(jax.ShapeDtypeStruct((128, 4096), bf16), jax.ShapeDtypeStruct((12, 4096), f32)),
        in_specs=[hbm, hbm, vmem, vmem],
        out_specs=(vmem, vmem),
        scratch_shapes=[
            pltpu.VMEM((BLOCKS, PIECES, 5, ROWS, COLS), bf16),
            pltpu.VMEM((PIECES, ROWS, 4096), bf16),
            pltpu.VMEM((4, 256, 384), bf16),
            pltpu.VMEM((2, 128, 384), bf16),
            pltpu.VMEM((BLOCKS, 256, COLS), f32),
            pltpu.VMEM((BLOCKS, 128, COLS), bf16),
            pltpu.VMEM((BLOCKS, 128, COLS), bf16),
            pltpu.VMEM((BLOCKS, 16, COLS), bf16),
            pltpu.VMEM((15, 16, COLS), bf16),
            pltpu.VMEM((4, 16, COLS), f32),
            pltpu.VMEM((3, 16, COLS), f32),
            pltpu.VMEM((BLOCKS, 16, COLS), f32),
            dma((4,)),
            dma((3,)),
            dma((3,)),
            dma((7,)),
            dma((7,)),
            dma((PIECES * 15,)),
            dma((PIECES * 15,)),
            dma((2 * PARTS,)),
            dma((2 * PARTS,)),
            dma((2 * PARTS,)),
            dma((2 * PARTS,)),
            dma((2 * PARTS,)),
            dma((2 * PARTS,)),
            dma((15,)),
            dma((15,)),
            dma((3,)),
            dma((3,)),
            dma((15,)),
            dma((15,)),
            dma((BLOCKS,)),
            dma((BLOCKS,)),
        ],
        compiler_params=pltpu.CompilerParams(
            collective_id=0, has_side_effects=True, vmem_limit_bytes=56 * 1024 * 1024
        ),
        cost_estimate=pl.CostEstimate(flops=2 * 256 * 1536 * 4096, bytes_accessed=8 << 20, transcendentals=0),
    )(attn_out, w_out.reshape(PIECES, ROWS, 4096), local_params.reshape(12, 4096), base_params)
    outer_grad = summed / lax.axis_size("replica")
    new_moment = moment_coef * moment + outer_grad
    new_params = (base_params.astype(f32) - outer_lr * (outer_grad + moment_coef * new_moment)).astype(bf16)
    return projected, new_params, new_moment


def solution(mesh):
    in_specs = (
        P("replica", "tensor"),
        P("tensor", None),
        P("replica", "tensor", None),
        P("tensor", None),
        P("tensor", None),
    )
    out_specs = (P(("replica", "tensor"), None), P("tensor", None), P("tensor", None))
    return jax.shard_map(local, mesh=mesh, in_specs=in_specs, out_specs=out_specs, check_vma=False)
```

time: 174 us -> 141 us (0.81)
  the two profiles are of different devices: /device:TPU:3 before, /device:TPU:711 now
where the time goes in v2:
time: 141 us; the launch traced here: 140 us
  Pallas kernels  136 us (96%)
  local copies, waits for them, and re-layouts  2.29 us (2%)
  other arithmetic  1.76 us (1%)
    pallas_call x1, Pallas kernels, local(): pl.pallas_call(kernel, out_shape=(jax.ShapeDtypeStruct((128, 4096), bf16)...  136 us

profile of v2, /device:TPU:711, one launch (start us, length us, event | category | flops | bytes accessed | tf_op | source)
XLA Modules:
  0.0 140.3 jit_solution(14333092214397130588)
XLA Ops:
  0.6 0.0 copy-start
  0.6 0.0 copy-start.1
  0.7 135.6 %shard_map.76 = (bf16[128,4096]{1,0:T(8,128)(2,1)}, f32[12,4096]{1,0:T(8,128)}) custom-call(bf16[1024,384]{1,0:T(8,128)(2,1)} %attn.1, bf16[8,48,4096]{2,1,0:T(8,128)(2,1)} %bitcast.2, bf16[12,4096]{1,0:T(8,128)(2,1)} %bitcast.3, bf16[12,4096]{1,0:T(8,128)(2,1)} %base.1), custom_call_target="tpu_custom_call" | custom-call | flops 3221225472 | bytes 8388608 | tf_op jit(solution)/shard_map/pallas_call | solution.py:373
  136.2 0.0 copy-done
  136.3 0.0 copy-done.1
  136.3 1.8 %subtract_convert_fusion = (bf16[12,4096]{1,0:T(8,128)(2,1)}, f32[12,4096]{1,0:T(8,128)}) fusion(bf16[12,4096]{1,0:T(8,128)(2,1)S(1)} %copy-done.1, f32[12,4096]{1,0:T(8,128)} %get-tuple-element.6, f32[12,4096]{1,0:T(8,128)S(1)} %copy-done), kind=kLoop, calls=%fused_computation | loop fusion | flops 442368 | bytes 786432 | tf_op jit(solution)/shard_map/convert_element_type | solution.py:420
  138.0 2.3 %copy.9 = bf16[128,4096]{1,0:T(8,128)(2,1)} copy(bf16[128,4096]{1,0:T(8,128)(2,1)} %get-tuple-element.12) | data formatting | bytes 2097152
Async XLA Ops:
  0.6 135.6 %copy-start = (f32[12,4096]{1,0:T(8,128)S(1)}, f32[12,4096]{1,0:T(8,128)}, u32[]{:S(2)}) copy-start(f32[12,4096]{1,0:T(8,128)} %param.9) | copy-start | bytes 589828
  0.6 135.6 %copy-start.1 = (bf16[12,4096]{1,0:T(8,128)(2,1)S(1)}, bf16[12,4096]{1,0:T(8,128)(2,1)}, u32[]{:S(2)}) copy-start(bf16[12,4096]{1,0:T(8,128)(2,1)} %base.1) | copy-start | bytes 294916

commit v3 on v2

--- a/solution.py
+++ b/solution.py
@@ -16,14 +16,14 @@
 OFFSETS = (0, -1, 1, 2)
 ROUNDS = PIECES + 2
 FAR_STEPS = (0, 1, 2, 3)
-NEAR_STEPS = (5, 6, 7, 8)
+NEAR_STEPS = (4, 6, 7, 8)
 UNROLL = 1
-RELAY_ROUNDS = (0, 1, 2, 3)
+RELAY_ROUNDS = (1, 2, 3, 4)
 PARTS = len(FAR_STEPS)
 
 
 def kernel(
-    attn, w, local_params, base, out, summed,
+    attn, w, local_hbm, base_hbm, out, summed, local_params, base,
     wall, own, heads, relay, acc, give, take, diff, diffs, zsum, ztake, grad,
     local_sem, first_send, first_recv, win_send, win_recv, plane_send, plane_recv,
     near_send, near_recv, far_send, far_recv, relay_send, relay_recv, diff_send, diff_recv, z_send, z_recv, grad_send, grad_recv, half_send, half_recv,
@@ -52,6 +52,8 @@
         pltpu.make_async_copy(w.at[:, :, columns], wall.at[mine, :, 4], local_sem.at[1]),
         pltpu.make_async_copy(w, own, local_sem.at[2]),
         pltpu.make_async_copy(attn.at[pl.ds(pl.multiple_of(z_hi * 256, 256), 256)], heads.at[0], local_sem.at[3]),
+        pltpu.make_async_copy(local_hbm, local_params, local_sem.at[4]),
+        pltpu.make_async_copy(base_hbm, base, local_sem.at[5]),
     ]
     for one in locals_:
         one.start()
@@ -62,7 +64,7 @@
 
     partners = [device(x + j % 4, y + j // 4, z, core) for j in range(1, 16)]
     partners += [device(x, y, z + 1, core), device(x, y, z - 1, core)]
-    partners += [device(x, y, z + 8 * j, core) for j in (1, 2, 3)]
+    partners += [device(x, y, z + 8, core), device(x, y, z - 8, core)]
     partners += [device(x, y, z_partner(step), core) for step in (1, 2)]
     sibling = device(x, y, z, 1 - core)
     partners += [sibling]
@@ -72,17 +74,23 @@
 
     pl.semaphore_wait(barrier, len(partners))
 
-    firsts = []
-    for j in (1, 2, 3):
-        firsts.append(
-            copy(
-                w.at[z_lo, :, columns], wall.at[mine, z_lo, 4 - j],
-                first_send.at[j - 1], first_recv.at[3 - j], device(x, y, z + 8 * j, core),
-            )
-        )
-        firsts[-1].start()
+    firsts = [
+        copy(
+            w.at[z_lo, :, columns], wall.at[mine, z_lo, 4 - j], first_send.at[j - 1], first_recv.at[j - 1],
+            device(x, y, z + 8 * j, core),
+        )
+        for j in (1, 3)
+    ]
+    for one in firsts:
+        one.start()
+    second = copy(
+        wall.at[mine, z_lo, 1 + 2 * core], wall.at[mine, z_lo, 2], first_send.at[1], first_recv.at[1],
+        device(x, y, z - 8 + 16 * core, core),
+    )
 
     diff[...] = jnp.zeros_like(diff)
+    locals_[4].wait()
+    locals_[5].wait()
 
     @pl.loop(0, BLOCKS)
     def _(block):
@@ -246,11 +254,13 @@
         total = total + diffs[j].astype(jnp.float32)
     zsum[0] = total
     z_copies[0].start()
+    for one in firsts:
+        one.wait_recv()
+    second.start()
     sum_step(0)
     locals_[0].wait()
     locals_[1].wait()
-    for one in firsts:
-        one.wait_recv()
+    second.wait_recv()
     window(z_lo, 1, True).start()
     window(z_lo, 2, False).start()
     stage0(0)
@@ -311,8 +321,18 @@
         for i in range(4):
             arrive(n, 5 + 3 * i)
 
+    @pl.loop(0, PIECES * 15)
+    def _(index):
+        part_ = wall.at[mine, 0, pl.ds(1, 3)]
+        copy(part_, part_, plane_send.at[index], plane_recv.at[index], sibling).wait_send()
+
+    for n in range(1, 8):
+        window(0, n, True).wait_send()
+    for one in firsts + [second] + diff_copies + far_copies + z_copies:
+        one.wait_send()
+
     for one in grad_copies:
-        one.wait_recv()
+        one.wait()
 
     @pl.loop(0, BLOCKS)
     def _(block):
@@ -326,10 +346,6 @@
 
     for one in near_copies:
         one.wait_recv()
-
-    @pl.loop(0, BLOCKS, unroll=UNROLL)
-    def _(block):
-        acc[block] += part(1, block) + part(3, block)
 
     for one in relays:
         one.wait_recv()
@@ -341,7 +357,7 @@
 
     @pl.loop(0, BLOCKS, unroll=UNROLL)
     def _(block):
-        acc[block] += part(2, block)
+        acc[block] += part(1, block) + part(2, block) + part(3, block)
         give[block] = acc[block, given, :].astype(jnp.bfloat16)
         half(block).start()
 
@@ -351,18 +367,11 @@
         half(block).wait_recv()
         out[:, at] = (acc[block, kept, :] + take[block].astype(jnp.float32)).astype(jnp.bfloat16)
 
-    @pl.loop(0, PIECES * 15)
-    def _(index):
-        part_ = wall.at[mine, 0, pl.ds(1, 3)]
-        copy(part_, part_, plane_send.at[index], plane_recv.at[index], sibling).wait_send()
-
     @pl.loop(0, BLOCKS)
     def _(block):
         half(block).wait_send()
 
-    for n in range(1, 8):
-        window(0, n, True).wait_send()
-    for one in firsts + diff_copies + near_copies + far_copies + relays + z_copies + grad_copies:
+    for one in near_copies + relays:
         one.wait_send()
 
 
@@ -373,9 +382,11 @@
     projected, summed = pl.pallas_call(
         kernel,
         out_shape=(jax.ShapeDtypeStruct((128, 4096), bf16), jax.ShapeDtypeStruct((12, 4096), f32)),
-        in_specs=[hbm, hbm, vmem, vmem],
+        in_specs=[hbm, hbm, hbm, hbm],
         out_specs=(vmem, vmem),
         scratch_shapes=[
+            pltpu.VMEM((12, 4096), bf16),
+            pltpu.VMEM((12, 4096), bf16),
             pltpu.VMEM((BLOCKS, PIECES, 5, ROWS, COLS), bf16),
             pltpu.VMEM((PIECES, ROWS, 4096), bf16),
             pltpu.VMEM((4, 256, 384), bf16),
@@ -388,7 +399,7 @@
             pltpu.VMEM((4, 16, COLS), f32),
             pltpu.VMEM((3, 16, COLS), f32),
             pltpu.VMEM((BLOCKS, 16, COLS), f32),
-            dma((4,)),
+            dma((6,)),
             dma((3,)),
             dma((3,)),
             dma((7,)),

time: 141 us -> 137 us (0.972)
  the two profiles are of different devices: /device:TPU:711 before, /device:TPU:31 now
where the time goes in v3:
time: 137 us; the launch traced here: 136 us
  Pallas kernels  132 us (96%)
  local copies, waits for them, and re-layouts  2.29 us (2%)
  other arithmetic  1.76 us (1%)
    pallas_call x1, Pallas kernels, local(): pl.pallas_call(kernel, out_shape=(jax.ShapeDtypeStruct((128, 4096), bf16)...  132 us

profile of v3, /device:TPU:31, one launch (start us, length us, event | category | flops | bytes accessed | tf_op | source)
XLA Modules:
  0.0 136.4 jit_solution(10882347605222615889)
XLA Ops:
  0.6 0.0 copy-start
  0.6 0.0 copy-start.1
  0.7 131.7 %shard_map.76 = (bf16[128,4096]{1,0:T(8,128)(2,1)}, f32[12,4096]{1,0:T(8,128)}) custom-call(bf16[1024,384]{1,0:T(8,128)(2,1)} %attn.1, bf16[8,48,4096]{2,1,0:T(8,128)(2,1)} %bitcast.2, bf16[12,4096]{1,0:T(8,128)(2,1)} %bitcast.3, bf16[12,4096]{1,0:T(8,128)(2,1)} %base_hbm.1), custom_call_target="tpu_custom_call" | custom-call | flops 3221225472 | bytes 8388608 | tf_op jit(solution)/shard_map/pallas_call | solution.py:382
  132.4 0.0 copy-done
  132.4 0.0 copy-done.1
  132.4 1.8 %subtract_convert_fusion = (bf16[12,4096]{1,0:T(8,128)(2,1)}, f32[12,4096]{1,0:T(8,128)}) fusion(bf16[12,4096]{1,0:T(8,128)(2,1)S(1)} %copy-done.1, f32[12,4096]{1,0:T(8,128)} %get-tuple-element.6, f32[12,4096]{1,0:T(8,128)S(1)} %copy-done), kind=kLoop, calls=%fused_computation | loop fusion | flops 442368 | bytes 786432 | tf_op jit(solution)/shard_map/convert_element_type | solution.py:431
  134.1 2.3 %copy.9 = bf16[128,4096]{1,0:T(8,128)(2,1)} copy(bf16[128,4096]{1,0:T(8,128)(2,1)} %get-tuple-element.12) | data formatting | bytes 2097152
Async XLA Ops:
  0.6 131.7 %copy-start = (f32[12,4096]{1,0:T(8,128)S(1)}, f32[12,4096]{1,0:T(8,128)}, u32[]{:S(2)}) copy-start(f32[12,4096]{1,0:T(8,128)} %param.9) | copy-start | bytes 589828
  0.6 131.7 %copy-start.1 = (bf16[12,4096]{1,0:T(8,128)(2,1)S(1)}, bf16[12,4096]{1,0:T(8,128)(2,1)}, u32[]{:S(2)}) copy-start(bf16[12,4096]{1,0:T(8,128)(2,1)} %base_hbm.1) | copy-start | bytes 294916
